TPU v7x, 32 devices: a whole 2x2x4 slice. The times are simulated.
32 devices in a mesh: wide: 16 (over z, y, core), narrow: 2 (over x).
Axes of the slice: x: 2, y: 2, z: 4, core: 2. Of those that a mesh axis runs over, the one named last changes fastest.
Arguments:
- tile_values: bfloat16 [224, 512, 512], P(('wide', 'narrow')), may hold values from -0.25 to 0.25
- tile_row: int32 [224], P(('wide', 'narrow')), may hold values from 0 to 1
- tile_col: int32 [224], P(('wide', 'narrow')), may hold values from 0 to 1
- basis: float32 [32768, 256], P(('wide', 'narrow')), may hold values from -6 to 6
Outputs:
- next_basis: float32 [1024, 256], P('wide')
All inputs are finite; a program needn't handle non-finite values.
Results may differ from a plain program's by a relative error of at most 0.0032.
Values sent between devices are 32-bit elements; how exact they have to be, the bound alone decides.
A program may use at most 64 MiB of HBM per device.

v0:
```python
import jax
import jax.numpy as jnp
from jax import lax
from jax.sharding import PartitionSpec as P

COLS_DEV = 64


def finish(owned_rows, gram_sum):
    factor = jnp.linalg.cholesky(gram_sum)
    return jax.scipy.linalg.solve_triangular(factor, owned_rows.T, lower=True).T


def gram_terms(owned_rows):
    return jnp.dot(
        owned_rows.T,
        owned_rows,
        precision=lax.Precision.HIGHEST,
        preferred_element_type=jnp.float32,
    )


def body(tile_values, tile_row, tile_col, basis):
    tile_edge = tile_values.shape[1]
    basis_width = basis.shape[1]
    blocks = basis.astype(jnp.bfloat16).reshape(basis.shape[0] // tile_edge, tile_edge, basis_width)
    chosen = jnp.take(blocks, tile_row, axis=0)
    products = jnp.einsum("tij,tik->tjk", tile_values, chosen, preferred_element_type=jnp.float32)
    col_blocks = COLS_DEV * lax.axis_size("wide") // tile_edge
    one_hot = (tile_col[None, :] == jnp.arange(col_blocks, dtype=jnp.int32)[:, None]).astype(
        jnp.float32
    )
    partial_value = jnp.einsum("ct,tjk->cjk", one_hot, products, precision=lax.Precision.HIGHEST)
    total_rows = col_blocks * tile_edge
    partial_value = partial_value.reshape(total_rows, basis_width)
    reduced = lax.psum_scatter(partial_value, "wide", scatter_dimension=0, tiled=True)
    owned_rows = lax.psum(reduced, "narrow")
    gram_sum = lax.psum(gram_terms(owned_rows), "wide") / total_rows
    return finish(owned_rows, gram_sum)


def solution(mesh):
    in_specs = (
        P(("wide", "narrow"), None, None),
        P(("wide", "narrow")),
        P(("wide", "narrow")),
        P(("wide", "narrow"), None),
    )
    out_specs = P("wide", None)
    return jax.shard_map(body, mesh=mesh, in_specs=in_specs, out_specs=out_specs, check_vma=False)
```

profile of v0, /device:TPU:0, one launch (start us, length us, event | category | flops | bytes accessed | tf_op | source)
XLA Modules:
  0.0 270.3 jit_solution(5383673118328847258)
XLA Ops:
  6.5 0.7 compare_select_fusion
  7.2 0.7 compare_and_fusion
  7.9 1.3 convert_element_type.4
  9.2 0.7 gather_fusion
  9.8 5.1 %fusion.2 = f32[7,256,512]{2,1,0:T(8,128)} fusion(bf16[7,512,512]{2,1,0:T(8,128)(2,1)} %param.4, bf16[7,512,256]{2,1,0:T(8,128)(2,1)S(1)} %gather_fusion, pred[7]{0:T(512)(128)(4,1)S(1)} %compare_and_fusion), kind=kOutput, calls=%fused_computation.5 | convolution fusion | flops 940441600 | bytes 9175047 | tf_op jit(solution)/shard_map/tij,tik->tjk/dot_general | solution.py:28
  15.0 5.3 %copy.10 = f32[7,256,512]{1,0,2:T(8,128)} copy(f32[7,256,512]{2,1,0:T(8,128)} %fusion.2) | data formatting | bytes 7340032 | tf_op jit(solution)/shard_map/tij,tik->tjk/dot_general | solution.py:28
  20.2 4.2 %fusion = f32[2,512,256]{2,0,1:T(2,128)S(1)} fusion(f32[7,256,512]{1,0,2:T(8,128)} %copy.10, s32[7]{0:T(128)S(1)} %copy-done.1), kind=kOutput, calls=%fused_computation.3 | convolution fusion | flops 22020110 | bytes 4718620 | tf_op jit(solution)/shard_map/ct,tjk->cjk/dot_general | solution.py:33
  24.5 1.1 copy.7
  25.6 60.3 %reduce-scatter.2.cloned.1.call-done = f32[64,256]{1,0:T(8,128)} async-done(((f32[1024,256]{1,0:T(8,128)}), f32[64,256]{1,0:T(8,128)}) %reduce-scatter.2.cloned.1.call-update) | async-done | bytes 65552 | tf_op jit(solution)/shard_map/reduce_scatter | solution.py:36
  85.9 0.2 all-reduce.6.cloned.1.call-start
  86.1 21.8 %all-reduce.4.cloned.1.call-done = f32[64,256]{1,0:T(8,128)} async-done(((f32[64,256]{1,0:T(8,128)}), f32[64,256]{1,0:T(8,128)}) %all-reduce.4.cloned.1.call-update) | async-done | bytes 65552 | tf_op jit(solution)/shard_map/psum | solution.py:37
  108.0 2.1 fusion.20
  110.1 90.4 %all-reduce.6.cloned.1.call-done = f32[256,256]{0,1:T(8,128)} async-done(((f32[256,256]{0,1:T(8,128)}), f32[256,256]{0,1:T(8,128)}) %all-reduce.6.cloned.1.call-update) | async-done | bytes 262160 | tf_op jit(solution)/shard_map/psum | solution.py:38
  200.5 1.0 broadcast_multiply_fusion
  201.5 0.1 copy.9
  201.6 1.0 fusion.6
  202.6 11.7 %cholesky.50 = f32[128,128]{1,0:T(8,128)S(1)} custom-call(f32[128,128]{1,0:T(8,128)S(1)} %cholesky.118), custom_call_target="Cholesky" | custom-call | tf_op jit(solution)/shard_map/jit(cholesky)/cholesky | solution.py:10
  214.4 9.8 %custom-call.15 = f32[1,128,128]{1,2,0:T(8,128)S(1)} custom-call(f32[1,128,128]{2,1,0:T(8,128)S(1)} %get-tuple-element.26), custom_call_target="InvertDiagBlocksLowerTriangular" | custom-call | tf_op jit(solution)/shard_map/jit(cholesky)/cholesky | solution.py:10
  224.2 0.2 constant_dynamic-update-slice_fusion.1
  224.4 0.3 convolution_subtract_fusion
  224.7 11.7 %cholesky.105 = f32[128,128]{1,0:T(8,128)S(1)} custom-call(f32[128,128]{1,0:T(8,128)S(1)} %convolution_subtract_fusion), custom_call_target="Cholesky" | custom-call | tf_op jit(solution)/shard_map/jit(cholesky)/cholesky | solution.py:10
  236.5 0.7 compare_reduce_fusion
  238.5 4.2 %while.1 = (s32[]{:T(128)}, f32[256,256]{1,0:T(8,128)S(1)}, s32[2,2]{1,0:T(2,128)S(1)}, f32[2,128,128]{2,1,0:T(8,128)S(1)}, s32[]{:T(128)}) while((s32[]{:T(128)}, f32[256,256]{1,0:T(8,128)S(1)}, s32[2,2]{1,0:T(2,128)S(1)}, f32[2,128,128]{2,1,0:T(8,128)S(1)}, s32[]{:T(128)}) %tuple.23), condition=%wide.while_cond, body=%wide.while_body.sunk | while | flops 2 | bytes 131181 | solution.py:11
  238.7 0.7 fusion.29
  239.4 1.3 bitcast_dynamic-update-slice_fusion.2
  240.8 0.7 fusion.29
  241.4 1.3 bitcast_dynamic-update-slice_fusion.2
  242.8 19.7 %custom-call.16 = f32[2,128,128]{1,2,0:T(8,128)S(1)} custom-call(f32[2,128,128]{2,1,0:T(8,128)S(1)} %get-tuple-element.12), custom_call_target="InvertDiagBlocksLowerTriangular" | custom-call | tf_op jit(solution)/shard_map/jit(_solve_triangular)/triangular_solve | solution.py:11
  262.5 0.2 fusion.9
  262.7 0.2 convolution_subtract_fusion.1
  262.9 0.2 fusion.8
  263.1 0.6 maximum_bitcast_fusion
  (20 shorter events, 0.3 us)
Async XLA Ops:
  6.5 79.4 %reduce-scatter.2.cloned.1.call-start = ((), (), s32[]{:S(2)}) async-start(), calls=%async_computation.1 | async-start | bytes 1114112 | tf_op jit(solution)/shard_map/reduce_scatter | solution.py:36
  15.0 5.3 %copy-start.1 = (s32[7]{0:T(128)S(1)}, s32[7]{0:T(128)}, u32[]{:S(2)}) copy-start(s32[7]{0:T(128)} %param.6) | copy-start | bytes 88
  25.6 82.4 %all-reduce.4.cloned.1.call-start = ((), (), s32[]{:S(2)}) async-start(), calls=%async_computation.2 | async-start | bytes 131072 | tf_op jit(solution)/shard_map/psum | solution.py:37
  85.9 114.6 %all-reduce.6.cloned.1.call-start = ((), (), s32[]{:S(2)}) async-start(), calls=%async_computation.3 | async-start | bytes 524288 | tf_op jit(solution)/shard_map/psum | solution.py:38
  108.0 154.5 %copy-start = (f32[64,256]{1,0:T(8,128)S(1)}, f32[64,256]{1,0:T(8,128)}, u32[]{:S(2)}) copy-start(f32[64,256]{1,0:T(8,128)} %all-reduce.4.cloned.1.call-done) | copy-start | bytes 196612
Sparse Core Ops, SparseCore 0:
  25.7 60.1 reduce-scatter.1
  88.2 19.7 all-reduce.3
  111.8 88.7 all-reduce.5
where the time goes:
time: 271 us; the launch traced here: 270 us
  waiting for transfers between devices  173 us (64%)
  other arithmetic  58.9 us (22%)
  between operations  14.5 us (5%)
  matrix products  12.5 us (5%)
  local copies, waits for them, and re-layouts  11.3 us (4%)
    psum x1, waiting for transfers between devices, body(): gram_sum = lax.psum(gram_terms(owned_rows), 'wide') / total_rows  90.4 us
    reduce_scatter x1, waiting for transfers between devices, body(): lax.psum_scatter(partial_value, 'wide', scatter_dimension=0, tiled=True)  60.3 us
    another operation x6, other arithmetic, finish(): factor = jnp.linalg.cholesky(gram_sum)  34 us
    psum x1, waiting for transfers between devices, body(): owned_rows = lax.psum(reduced, 'narrow')  21.8 us
    another operation x3, other arithmetic, finish(): return jax.scipy.linalg.solve_triangular(factor, owned_rows.T, lower=True).T  19.7 us
  transfers between devices with their start and end apart: 3, of which 3 were waited for; matrix products, arithmetic and copies ran while one was open for 0% of the time, Pallas kernels for 0%

commit v1 on v0

v1 whole, which is shorter than its diff:
```python
import functools

import jax
import jax.numpy as jnp
from jax import lax
from jax.experimental import pallas as pl
from jax.experimental.pallas import tpu as pltpu
from jax.sharding import PartitionSpec as P

MESH = pl.DeviceIdType.MESH
HIGHEST = lax.Precision.HIGHEST
VMEM_LIMIT = 48 * 1024 * 1024
COLS_DEV = 64


def local_kernel(row_ref, col_ref, tile_ref, basis_ref, out_ref, rounded):
    t = pl.program_id(0)
    edge = tile_ref.shape[1]

    @pl.when(t == 0)
    def _():
        rounded[...] = basis_ref[...].astype(jnp.bfloat16)
        out_ref[...] = jnp.zeros_like(out_ref)

    r = pl.multiple_of(row_ref[t] * edge, edge)
    c = pl.multiple_of(col_ref[t] * edge, edge)
    out_ref[pl.ds(c, edge), :] += lax.dot_general(
        tile_ref[0],
        rounded[pl.ds(r, edge), :],
        (((0,), (0,)), ((), ())),
        preferred_element_type=jnp.float32,
    )


def local_terms(tile_values, tile_row, tile_col, basis, total_rows):
    tiles, edge, _ = tile_values.shape
    rows, rank = basis.shape
    return pl.pallas_call(
        local_kernel,
        out_shape=jax.ShapeDtypeStruct((total_rows, rank), jnp.float32),
        grid_spec=pltpu.PrefetchScalarGridSpec(
            num_scalar_prefetch=2,
            grid=(tiles,),
            in_specs=[
                pl.BlockSpec((1, edge, edge), lambda t, *_: (t, 0, 0)),
                pl.BlockSpec((rows, rank), lambda t, *_: (0, 0)),
            ],
            out_specs=pl.BlockSpec((total_rows, rank), lambda t, *_: (0, 0)),
            scratch_shapes=[pltpu.VMEM((rows, rank), jnp.bfloat16)],
        ),
        compiler_params=pltpu.CompilerParams(vmem_limit_bytes=VMEM_LIMIT),
    )(tile_row, tile_col, tile_values, basis)


def stream_orders(n_wide, n_narrow, chunk_rows):
    nb = n_narrow.bit_length() - 1
    wb = n_wide.bit_length() - 1
    core = [nb]
    narrow = list(range(nb))
    rest = [nb + i for i in range(1, wb)]
    first = core + narrow + rest
    second = core + rest[:1] + narrow + rest[1:]
    return [first, second] if chunk_rows % 16 == 0 else [first]


def split_sizes(order, step):
    left = sorted(order[step:])
    at = left.index(order[step])
    return 2 ** (len(left) - 1 - at), 2**at


def sum_gather_kernel(n_narrow, orders, part_ref, *refs):
    out_refs = refs[: len(orders)]
    recv0, recvs, accs, send_sem, recv_sem, gsend_sem, grecv_sem = refs[len(orders) :]
    w, n = lax.axis_index("wide"), lax.axis_index("narrow")
    me = w * n_narrow + n
    steps = len(orders[0])
    streams = len(orders)
    rows = out_refs[0].shape[1]

    def bit(b):
        return (me // (2**b)) % 2

    def partner(b):
        other = me + (1 - 2 * bit(b)) * (2**b)
        return (other // n_narrow, other % n_narrow)

    barrier = pltpu.get_barrier_semaphore()
    for b in range(steps):
        pl.semaphore_signal(barrier, inc=1, device_id=partner(b), device_id_type=MESH)
    pl.semaphore_wait(barrier, steps)

    b = orders[0][0]
    mine = bit(b)
    copy = pltpu.make_async_remote_copy(
        src_ref=part_ref.at[:, 1 - mine],
        dst_ref=recv0,
        send_sem=send_sem.at[0, 0],
        recv_sem=recv_sem.at[0, 0],
        device_id=partner(b),
        device_id_type=MESH,
    )
    copy.start()
    copy.wait()
    for s in range(streams):
        lanes = pl.ds(s * rows, rows)
        both = part_ref[:, pl.ds(mine, 1), :, lanes][:, 0] + recv0[:, :, lanes]
        accs[s][0][...] = both.reshape(accs[s][0].shape)

    copies = [None] * streams
    for step in range(1, steps):
        for s in range(streams):
            b = orders[s][step]
            copies[s] = pltpu.make_async_remote_copy(
                src_ref=accs[s][step - 1].at[:, 1 - bit(b)],
                dst_ref=recvs[s][step - 1],
                send_sem=send_sem.at[step, s],
                recv_sem=recv_sem.at[step, s],
                device_id=partner(b),
                device_id_type=MESH,
            )
            copies[s].start()
        for s in range(streams):
            mine = bit(orders[s][step])
            copies[s].wait()
            both = accs[s][step - 1][:, pl.ds(mine, 1)][:, 0] + recvs[s][step - 1][...]
            if step < steps - 1:
                accs[s][step][...] = both.reshape(accs[s][step].shape)
            else:
                place = place_of(orders[s], w, n, n_narrow)
                out_refs[s][pl.ds(place, 1)] = both.reshape((1,) + out_refs[s].shape[1:])

    for i in range(steps):
        for s in range(streams):
            b = orders[s][steps - 1 - i]
            place = place_of(orders[s], w, n, n_narrow)
            size = 2**i
            block = out_refs[s].at[pl.ds((place // size) * size, size)]
            copies[s] = pltpu.make_async_remote_copy(
                src_ref=block,
                dst_ref=block,
                send_sem=gsend_sem.at[i, s],
                recv_sem=grecv_sem.at[i, s],
                device_id=partner(b),
                device_id_type=MESH,
            )
            copies[s].start()
        for s in range(streams):
            copies[s].wait()


def place_of(order, w, n, n_narrow):
    number = w * n_narrow + n
    place = 0
    for i, b in enumerate(reversed(order)):
        place = place + ((number // (2**b)) % 2) * (2**i)
    return place


def sum_and_gather(partial, n_wide, n_narrow):
    total_rows, rank = partial.shape
    devices = n_wide * n_narrow
    chunk = total_rows // devices
    orders = stream_orders(n_wide, n_narrow, chunk)
    steps, streams = len(orders[0]), len(orders)
    rows = chunk // streams
    hi, lo = split_sizes(orders[0], 0)
    recvs, accs = [], []
    for order in orders:
        recv, acc = [], []
        for step in range(1, steps):
            up, down = split_sizes(order, step)
            acc.append(pltpu.VMEM((up, 2, down, rows, rank), jnp.float32))
            recv.append(pltpu.VMEM((up, down, rows, rank), jnp.float32))
        recvs.append(recv)
        accs.append(acc)
    block = pl.BlockSpec(memory_space=pltpu.VMEM)
    sems = pltpu.SemaphoreType.DMA((steps, streams))
    return pl.pallas_call(
        functools.partial(sum_gather_kernel, n_narrow, orders),
        out_shape=[jax.ShapeDtypeStruct((devices, rows, rank), jnp.float32)] * streams,
        in_specs=[block],
        out_specs=[block] * streams,
        scratch_shapes=[pltpu.VMEM((hi, lo, chunk, rank), jnp.float32), recvs, accs, sems, sems, sems, sems],
        compiler_params=pltpu.CompilerParams(collective_id=0, has_side_effects=True, vmem_limit_bytes=VMEM_LIMIT),
    )(partial.reshape(hi, 2, lo, chunk, rank)), orders


LANES = 128
PANEL = 8
OUTER = 32


def splat(value):
    return jnp.broadcast_to(value, (PANEL, LANES))


def finish_kernel(orders, n_narrow, *refs):
    streams = len(orders)
    y_refs, out_ref, work = refs[:streams], refs[streams], refs[streams + 1]
    devices, rows, rank = y_refs[0].shape
    owned = out_ref.shape[0]
    total_rows = devices * rows * streams
    width = work.shape[1]
    w = lax.axis_index("wide")

    gram = jnp.zeros((rank, rank), jnp.float32)
    for s in range(streams):
        flat = y_refs[s][...].reshape(devices * rows, rank)
        gram += lax.dot_general(
            flat, flat, (((0,), (0,)), ((), ())), precision=HIGHEST, preferred_element_type=jnp.float32
        )
    work[:, :rank] = gram * (1.0 / total_rows)
    pieces = []
    for n in range(n_narrow):
        for s in range(streams):
            pieces.append(y_refs[s][place_of(orders[s], w, n, n_narrow)])
    pieces.append(jnp.zeros((width - rank - owned, rank), jnp.float32))
    work[:, rank:] = jnp.concatenate(pieces, axis=0).T

    for outer in range(0, rank, OUTER):
        base = (outer // LANES) * LANES
        blocks = list(range(base, width, LANES))
        groups = [
            [work[outer + g : outer + g + PANEL, c : c + LANES] for c in blocks] for g in range(0, OUTER, PANEL)
        ]
        for p in range(OUTER // PANEL):
            k = outer + p * PANEL - base
            head = groups[p][0]
            cols = [splat(head[:, k + j : k + j + 1]) for j in range(PANEL)]
            entry = [[splat(cols[j][i : i + 1, :]) for j in range(i + 1)] for i in range(PANEL)]
            scale = []
            for j in range(PANEL):
                scale.append(lax.rsqrt(entry[j][j]))
                for i in range(j + 1, PANEL):
                    entry[i][j] = entry[i][j] * scale[j]
                for i in range(j + 1, PANEL):
                    for m in range(j + 1, i + 1):
                        entry[i][m] = entry[i][m] - entry[i][j] * entry[m][j]
            solved = [[splat(block[j : j + 1, :]) for block in groups[p]] for j in range(PANEL)]
            for j in range(PANEL):
                solved[j] = [v * scale[j] for v in solved[j]]
                for i in range(j + 1, PANEL):
                    solved[i] = [a - entry[i][j] * v for a, v in zip(solved[i], solved[j])]
            place = lax.broadcasted_iota(jnp.int32, (PANEL, LANES), 0)
            final = solved[0]
            for j in range(1, PANEL):
                final = [jnp.where(place == j, v, f) for v, f in zip(solved[j], final)]
            for g in range(p + 1, OUTER // PANEL):
                low = groups[g][0]
                mult = [splat(low[:, k + j : k + j + 1]) for j in range(PANEL)]
                for j in range(PANEL):
                    mult[j] = mult[j] * scale[j]
                    for i in range(j + 1, PANEL):
                        mult[i] = mult[i] - entry[i][j] * mult[j]
                for j in range(PANEL):
                    groups[g] = [a - mult[j] * v for a, v in zip(groups[g], solved[j])]
            row = outer + p * PANEL
            for c, f in zip(blocks, final):
                work[row : row + PANEL, c : c + LANES] = f
        after = outer + OUTER
        if after < rank:
            start = (after // LANES) * LANES
            done = work[outer:after, start:]
            update = lax.dot_general(
                done[:, after - start : rank - start],
                done,
                (((0,), (0,)), ((), ())),
                precision=HIGHEST,
                preferred_element_type=jnp.float32,
            )
            work[after:rank, start:] -= update
    out_ref[...] = work[:, rank:].T[:owned]


def finish(gathered, orders, owned, n_narrow):
    rank = gathered[0].shape[-1]
    width = rank + -(-owned // LANES) * LANES
    return pl.pallas_call(
        functools.partial(finish_kernel, orders, n_narrow),
        out_shape=jax.ShapeDtypeStruct((owned, rank), jnp.float32),
        in_specs=[pl.BlockSpec(memory_space=pltpu.VMEM)] * len(gathered),
        out_specs=pl.BlockSpec(memory_space=pltpu.VMEM),
        scratch_shapes=[pltpu.VMEM((rank, width), jnp.float32)],
        compiler_params=pltpu.CompilerParams(vmem_limit_bytes=VMEM_LIMIT),
    )(*gathered)


def solution(mesh):
    n_wide, n_narrow = mesh.shape["wide"], mesh.shape["narrow"]
    owned = COLS_DEV

    def body(tile_values, tile_row, tile_col, basis):
        total_rows = owned * n_wide
        partial = local_terms(tile_values, tile_row, tile_col, basis, total_rows)
        gathered, orders = sum_and_gather(partial, n_wide, n_narrow)
        return finish(gathered, orders, owned, n_narrow)

    in_specs = (
        P(("wide", "narrow"), None, None),
        P(("wide", "narrow")),
        P(("wide", "narrow")),
        P(("wide", "narrow"), None),
    )
    return jax.shard_map(body, mesh=mesh, in_specs=in_specs, out_specs=P("wide", None), check_vma=False)
```

time: 271 us -> 57.9 us (0.21)
  waiting for transfers between devices: 173 us -> 0 us
  other arithmetic: 58.9 us -> 0 us
  Pallas kernels: 0 us -> 53.1 us
  between operations: 14.5 us -> 0.02 us
  matrix products: 12.5 us -> 0 us
  local copies, waits for them, and re-layouts: 11.3 us -> 4.57 us
    psum x2 -> x0, waiting for transfers between devices: 112 us -> none  [the longest x1 90.4 us: body(): gram_sum = lax.psum(gram_terms(owned_rows), 'wide') / total_rows]
    reduce_scatter x1 -> x0, waiting for transfers between devices: 60.3 us -> none  [body(): lax.psum_scatter(partial_value, 'wide', scatter_dimension=0, tiled=True)]
    another operation x9 -> x0, other arithmetic: 53.7 us -> none  [the longest x6 34 us: finish(): factor = jnp.linalg.cholesky(gram_sum)]
    pallas_call x0 -> x3, Pallas kernels: none -> 53.1 us  [the longest x1 38.2 us: sum_and_gather(): pl.pallas_call(functools.partial(sum_gather_kernel, n_narrow, orders), ou...]
    dot_general x3 -> x0, matrix products: 11.4 us -> none  [the longest x1 5.14 us: body(): jnp.einsum('tij,tik->tjk', tile_values, chosen, preferred_element_type=jn...]
    dot_general x2 -> x0, local copies, waits for them, and re-layouts: 6.35 us -> none  [the longest x1 5.27 us: body(): jnp.einsum('tij,tik->tjk', tile_values, chosen, preferred_element_type=jn...]
    unnamed x4 -> x8, local copies, waits for them, and re-layouts: 0.01 us -> 4.57 us
    another operation x9 -> x0, local copies, waits for them, and re-layouts: 4.12 us -> none
  transfers between devices with their start and end apart: 3 -> 0, of which waited for: 3 -> 0; matrix products, arithmetic and copies ran while one was open for 0% -> 0% of each run, Pallas kernels for 0% -> 0%
where the time goes in v1:
time: 57.9 us; the launch traced here: 57.7 us
  Pallas kernels  53.1 us (92%)
  local copies, waits for them, and re-layouts  4.57 us (8%)
    pallas_call x1, Pallas kernels, sum_and_gather(): pl.pallas_call(functools.partial(sum_gather_kernel, n_narrow, orders), ou...  38.2 us
    pallas_call x1, Pallas kernels, finish(): pl.pallas_call(functools.partial(finish_kernel, orders, n_narrow), out_sh...  11.7 us
    unnamed x8, local copies, waits for them, and re-layouts  4.57 us
    pallas_call x1, Pallas kernels, local_terms(): pl.pallas_call(local_kernel, out_shape=jax.ShapeDtypeStruct((total_rows,...  3.18 us

profile of v1, /device:TPU:0, one launch (start us, length us, event | category | flops | bytes accessed | tf_op | source)
XLA Modules:
  0.0 57.7 jit_solution(6143319198507685914)
XLA Ops:
  0.0 0.0 copy-start
  0.0 2.0 %copy-done = bf16[7,512,512]{2,1,0:T(8,128)(2,1)S(1)} copy-done((bf16[7,512,512]{2,1,0:T(8,128)(2,1)S(1)}, bf16[7,512,512]{2,1,0:T(8,128)(2,1)}, u32[]{:S(2)}) %copy-start) | copy-done | bytes 3670040
  2.0 0.0 copy-start.1
  2.0 1.2 %copy-done.1 = f32[1024,256]{1,0:T(8,128)S(1)} copy-done((f32[1024,256]{1,0:T(8,128)S(1)}, f32[1024,256]{1,0:T(8,128)}, u32[]{:S(2)}) %copy-start.1) | copy-done | bytes 1048600
  3.3 0.0 copy-start.2
  3.3 0.7 %copy-done.2 = s32[7]{0:T(128)S(1)} copy-done((s32[7]{0:T(128)S(1)}, s32[7]{0:T(128)}, u32[]{:S(2)}) %copy-start.2) | copy-done | bytes 52
  3.9 0.0 copy-start.3
  3.9 0.7 %copy-done.3 = s32[7]{0:T(128)S(1)} copy-done((s32[7]{0:T(128)S(1)}, s32[7]{0:T(128)}, u32[]{:S(2)}) %copy-start.3) | copy-done | bytes 52
  4.6 3.2 %shard_map.46 = f32[1024,256]{1,0:T(8,128)S(1)} custom-call(s32[7]{0:T(128)S(1)} %copy-done.2, s32[7]{0:T(128)S(1)} %copy-done.3, bf16[7,512,512]{2,1,0:T(8,128)(2,1)S(1)} %copy-done, f32[1024,256]{1,0:T(8,128)S(1)} %copy-done.1), custom_call_target="tpu_custom_call" | custom-call | tf_op jit(solution)/shard_map/pallas_call | solution.py:38
  7.8 38.2 %shard_map.47 = (f32[32,16,256]{2,1,0:T(8,128)S(1)}, f32[32,16,256]{2,1,0:T(8,128)S(1)}) custom-call(f32[8,2,2,32,256]{4,3,2,1,0:T(8,128)S(1)} %bitcast.1), custom_call_target="tpu_custom_call" | custom-call | tf_op jit(solution)/shard_map/pallas_call | solution.py:179
  45.9 11.7 %shard_map.48 = f32[64,256]{1,0:T(8,128)} custom-call(f32[32,16,256]{2,1,0:T(8,128)S(1)} %get-tuple-element.7.refs_0_, f32[32,16,256]{2,1,0:T(8,128)S(1)} %get-tuple-element.8.refs_1_), custom_call_target="tpu_custom_call" | custom-call | tf_op jit(solution)/shard_map/pallas_call | solution.py:279
Async XLA Ops:
  0.0 2.0 %copy-start = (bf16[7,512,512]{2,1,0:T(8,128)(2,1)S(1)}, bf16[7,512,512]{2,1,0:T(8,128)(2,1)}, u32[]{:S(2)}) copy-start(bf16[7,512,512]{2,1,0:T(8,128)(2,1)} %tile_ref.1) | copy-start | bytes 11010052
  2.0 1.2 %copy-start.1 = (f32[1024,256]{1,0:T(8,128)S(1)}, f32[1024,256]{1,0:T(8,128)}, u32[]{:S(2)}) copy-start(f32[1024,256]{1,0:T(8,128)} %basis_ref.1) | copy-start | bytes 3145732
  3.3 0.7 %copy-start.2 = (s32[7]{0:T(128)S(1)}, s32[7]{0:T(128)}, u32[]{:S(2)}) copy-start(s32[7]{0:T(128)} %row_ref.1) | copy-start | bytes 88
  3.9 0.7 %copy-start.3 = (s32[7]{0:T(128)S(1)}, s32[7]{0:T(128)}, u32[]{:S(2)}) copy-start(s32[7]{0:T(128)} %col_ref.1) | copy-start | bytes 88

commit v2 on v1

v2 whole, which is shorter than its diff:
```python
import functools

import jax
import jax.numpy as jnp
from jax import lax
from jax.experimental import pallas as pl
from jax.experimental.pallas import tpu as pltpu
from jax.sharding import PartitionSpec as P

MESH = pl.DeviceIdType.MESH
HIGHEST = lax.Precision.HIGHEST
VMEM_LIMIT = 48 * 1024 * 1024
COLS_DEV = 64
LANES = 128


def local_kernel(row_hbm, col_hbm, tile_hbm, basis_hbm, out_ref, row_ref, col_ref, tiles, basis, rounded, sem, tile_sem):
    count, edge, _ = tiles.shape
    small = [
        pltpu.make_async_copy(row_hbm, row_ref, sem.at[0]),
        pltpu.make_async_copy(col_hbm, col_ref, sem.at[1]),
        pltpu.make_async_copy(basis_hbm, basis, sem.at[2]),
    ]
    large = [pltpu.make_async_copy(tile_hbm.at[t], tiles.at[t], tile_sem.at[t]) for t in range(count)]
    for copy in small + large:
        copy.start()
    out_ref[...] = jnp.zeros_like(out_ref)
    for copy in small:
        copy.wait()
    rounded[...] = basis[...].astype(jnp.bfloat16)
    for t in range(count):
        large[t].wait()
        r = pl.multiple_of(row_ref[t] * edge, edge)
        c = pl.multiple_of(col_ref[t] * edge, edge)
        out_ref[pl.ds(c, edge), :] += lax.dot_general(
            tiles[t],
            rounded[pl.ds(r, edge), :],
            (((0,), (0,)), ((), ())),
            preferred_element_type=jnp.float32,
        )


def local_terms(tile_values, tile_row, tile_col, basis, total_rows):
    count = tile_values.shape[0]
    rows, rank = basis.shape
    return pl.pallas_call(
        local_kernel,
        out_shape=jax.ShapeDtypeStruct((total_rows, rank), jnp.float32),
        in_specs=[pl.BlockSpec(memory_space=pltpu.HBM)] * 4,
        out_specs=pl.BlockSpec(memory_space=pltpu.VMEM),
        scratch_shapes=[
            pltpu.SMEM((count,), jnp.int32),
            pltpu.SMEM((count,), jnp.int32),
            pltpu.VMEM(tile_values.shape, jnp.bfloat16),
            pltpu.VMEM((rows, rank), jnp.float32),
            pltpu.VMEM((rows, rank), jnp.bfloat16),
            pltpu.SemaphoreType.DMA((3,)),
            pltpu.SemaphoreType.DMA((count,)),
        ],
        compiler_params=pltpu.CompilerParams(vmem_limit_bytes=VMEM_LIMIT),
    )(tile_row, tile_col, tile_values, basis)


def stream_orders(n_wide, n_narrow, chunk_rows):
    nb = n_narrow.bit_length() - 1
    wb = n_wide.bit_length() - 1
    core = [(nb,)]
    narrow = [(i,) for i in range(nb)]
    second = [(nb + i,) for i in range(1, min(wb, 2))]
    rest = [tuple(range(nb + i, min(nb + i + 2, nb + wb))) for i in range(2, wb, 2)]
    pair = [core + narrow + second + rest, core + second + narrow + rest]
    if chunk_rows % 32 == 0:
        return pair + pair
    return pair if chunk_rows % 16 == 0 else pair[:1]


def split_sizes(order, step):
    left = sorted(b for group in order[step:] for b in group)
    at = left.index(order[step][0])
    size = len(order[step])
    return 2 ** (len(left) - at - size), 2**size, 2**at


def place_of(order, number):
    place, scale = 0, 1
    for group in reversed(order[1:]):
        place = place + ((number // 2 ** group[0]) % 2 ** len(group)) * scale
        scale = scale * 2 ** len(group)
    return place


def sum_gather_kernel(n_narrow, orders, part_ref, gram_ref, owned_ref, recvs, accs, rows_all, gram_own, gram_in, sems):
    w, n = lax.axis_index("wide"), lax.axis_index("narrow")
    me = w * n_narrow + n
    steps, streams = len(orders[0]), len(orders)
    rows, rank = rows_all.shape[2], rows_all.shape[3]
    send_sem, recv_sem, gather_send, gather_recv, gram_send, gram_recv = sems

    def partner(group, delta):
        other, digit = me, (me // 2 ** group[0]) % 2 ** len(group)
        for i, b in enumerate(group):
            if (delta >> i) & 1:
                turn = 1 - 2 * ((me // 2**b) % 2)
                other, digit = other + turn * 2**b, digit + turn * 2**i
        return {"wide": other // n_narrow, "narrow": other % n_narrow}, digit

    barrier = pltpu.get_barrier_semaphore()
    met = 0
    for group in orders[0]:
        for delta in range(1, 2 ** len(group)):
            device, _ = partner(group, delta)
            pl.semaphore_signal(barrier, inc=1, device_id=device, device_id_type=MESH)
            met += 1
    pl.semaphore_wait(barrier, met)

    def block_of(step, s, digit):
        if step == 0:
            return part_ref.at[:, digit, :, pl.ds(s * rows, rows)]
        return accs[s][step - 1].at[:, digit]

    def start_sum(step, s):
        group, copies = orders[s][step], []
        for delta in range(1, 2 ** len(group)):
            device, digit = partner(group, delta)
            copy = pltpu.make_async_remote_copy(
                src_ref=block_of(step, s, digit),
                dst_ref=recvs[s][step].at[delta - 1],
                send_sem=send_sem.at[step, s, delta - 1],
                recv_sem=recv_sem.at[step, s, delta - 1],
                device_id=device,
                device_id_type=MESH,
            )
            copy.start()
            copies.append(copy)
        return copies

    def start_gather(step, s):
        group, copies = orders[s][step], []
        size = 1
        for later in orders[s][step + 1 :]:
            size = size * 2 ** len(later)
        place = place_of(orders[s], me)
        block = rows_all.at[s, pl.ds((place // size) * size, size)]
        for delta in range(1, 2 ** len(group)):
            device, _ = partner(group, delta)
            copy = pltpu.make_async_remote_copy(
                src_ref=block,
                dst_ref=block,
                send_sem=gather_send.at[step, s, delta - 1],
                recv_sem=gather_recv.at[step, s, delta - 1],
                device_id=device,
                device_id_type=MESH,
            )
            copy.start()
            copies.append(copy)
        return copies

    flying = [start_sum(0, s) for s in range(streams)]
    for step in range(steps):
        for s in range(streams):
            group = orders[s][step]
            digit = (me // 2 ** group[0]) % 2 ** len(group)
            total = block_of(step, s, digit)[...]
            for delta, copy in enumerate(flying[s]):
                copy.wait()
                total = total + recvs[s][step][delta]
            if step < steps - 1:
                accs[s][step][...] = total.reshape(accs[s][step].shape)
                flying[s] = start_sum(step + 1, s)
            else:
                rows_all[s, pl.ds(place_of(orders[s], me), 1)] = total.reshape((1, rows, rank))
                flying[s] = start_gather(step, s)
    for step in range(steps - 1, 0, -1):
        for s in range(streams):
            for copy in flying[s]:
                copy.wait()
            if step > 1:
                flying[s] = start_gather(step - 1, s)

    held = rows_all[...].reshape(-1, rank)
    device, _ = partner(orders[0][0], 1)
    copies = []
    for i, at in enumerate(range(0, rank, LANES)):
        place = (slice(at, at + LANES), slice(at, rank))
        gram_own[place] = lax.dot_general(
            held[:, at : at + LANES],
            held[:, at:],
            (((0,), (0,)), ((), ())),
            precision=HIGHEST,
            preferred_element_type=jnp.float32,
        )
        copy = pltpu.make_async_remote_copy(
            src_ref=gram_own.at[pl.ds(at, LANES), pl.ds(at, rank - at)],
            dst_ref=gram_in.at[pl.ds(at, LANES), pl.ds(at, rank - at)],
            send_sem=gram_send.at[i],
            recv_sem=gram_recv.at[i],
            device_id=device,
            device_id_type=MESH,
        )
        copy.start()
        copies.append(copy)
    for other in range(n_narrow):
        for s in range(streams):
            at = (other * streams + s) * rows
            owned_ref[at : at + rows, :] = rows_all[s, place_of(orders[s], w * n_narrow + other)]
    for at, copy in zip(range(0, rank, LANES), copies):
        copy.wait()
        place = (slice(at, at + LANES), slice(at, rank))
        gram_ref[place] = gram_own[place] + gram_in[place]
        if at > 0:
            gram_ref[at : at + LANES, :at] = jnp.zeros((LANES, at), jnp.float32)


def sum_and_gather(partial, n_wide, n_narrow):
    total_rows, rank = partial.shape
    devices = n_wide * n_narrow
    chunk = total_rows // devices
    orders = stream_orders(n_wide, n_narrow, chunk)
    steps, streams = len(orders[0]), len(orders)
    rows = chunk // streams
    recvs, accs = [], []
    for order in orders:
        recv, acc = [], []
        for step in range(steps):
            up, size, down = split_sizes(order, step)
            recv.append(pltpu.VMEM((size - 1, up, down, rows, rank), jnp.float32))
            if step > 0:
                acc.append(pltpu.VMEM((up, size, down, rows, rank), jnp.float32))
        recvs.append(recv)
        accs.append(acc)
    up, size, down = split_sizes(orders[0], 0)
    block = pl.BlockSpec(memory_space=pltpu.VMEM)
    most = max(2 ** len(group) for group in orders[0]) - 1
    sems = [pltpu.SemaphoreType.DMA((steps, streams, most))] * 4 + [pltpu.SemaphoreType.DMA((rank // LANES,))] * 2
    square = pltpu.VMEM((rank, rank), jnp.float32)
    return pl.pallas_call(
        functools.partial(sum_gather_kernel, n_narrow, orders),
        out_shape=[
            jax.ShapeDtypeStruct((rank, rank), jnp.float32),
            jax.ShapeDtypeStruct((chunk * n_narrow, rank), jnp.float32),
        ],
        in_specs=[block],
        out_specs=[block] * 2,
        scratch_shapes=[
            recvs,
            accs,
            pltpu.VMEM((streams, devices // 2, rows, rank), jnp.float32),
            square,
            square,
            sems,
        ],
        compiler_params=pltpu.CompilerParams(collective_id=0, has_side_effects=True, vmem_limit_bytes=VMEM_LIMIT),
    )(partial.reshape(up, size, down, chunk, rank))


PANEL = 8
OUTER = 32


def splat(value):
    return jnp.broadcast_to(value, (PANEL, LANES))


def finish_kernel(total_rows, gram_ref, owned_ref, out_ref, work):
    owned, rank = owned_ref.shape
    width = work.shape[1]
    work[:, :rank] = gram_ref[...] * (1.0 / total_rows)
    filled = jnp.concatenate([owned_ref[...], jnp.zeros((width - rank - owned, rank), jnp.float32)], axis=0)
    work[:, rank:] = filled.T

    for outer in range(0, rank, OUTER):
        base = (outer // LANES) * LANES
        blocks = list(range(base, width, LANES))
        groups = [
            [work[outer + g : outer + g + PANEL, c : c + LANES] for c in blocks] for g in range(0, OUTER, PANEL)
        ]
        for p in range(OUTER // PANEL):
            k = outer + p * PANEL - base
            head = groups[p][0]
            cols = [splat(head[:, k + j : k + j + 1]) for j in range(PANEL)]
            entry = [[splat(cols[j][i : i + 1, :]) for j in range(i + 1)] for i in range(PANEL)]
            scale = []
            for j in range(PANEL):
                scale.append(lax.rsqrt(entry[j][j]))
                for i in range(j + 1, PANEL):
                    entry[i][j] = entry[i][j] * scale[j]
                for i in range(j + 1, PANEL):
                    for m in range(j + 1, i + 1):
                        entry[i][m] = entry[i][m] - entry[i][j] * entry[m][j]
            solved = [[splat(block[j : j + 1, :]) for block in groups[p]] for j in range(PANEL)]
            for j in range(PANEL):
                solved[j] = [v * scale[j] for v in solved[j]]
                for i in range(j + 1, PANEL):
                    solved[i] = [a - entry[i][j] * v for a, v in zip(solved[i], solved[j])]
            place = lax.broadcasted_iota(jnp.int32, (PANEL, LANES), 0)
            final = solved[0]
            for j in range(1, PANEL):
                final = [jnp.where(place == j, v, f) for v, f in zip(solved[j], final)]
            for g in range(p + 1, OUTER // PANEL):
                low = groups[g][0]
                mult = [splat(low[:, k + j : k + j + 1]) for j in range(PANEL)]
                for j in range(PANEL):
                    mult[j] = mult[j] * scale[j]
                    for i in range(j + 1, PANEL):
                        mult[i] = mult[i] - entry[i][j] * mult[j]
                for j in range(PANEL):
                    groups[g] = [a - mult[j] * v for a, v in zip(groups[g], solved[j])]
            row = outer + p * PANEL
            for c, f in zip(blocks, final):
                work[row : row + PANEL, c : c + LANES] = f
        after = outer + OUTER
        if after < rank:
            start = (after // LANES) * LANES
            done = work[outer:after, start:]
            update = lax.dot_general(
                done[:, after - start : rank - start],
                done,
                (((0,), (0,)), ((), ())),
                precision=HIGHEST,
                preferred_element_type=jnp.float32,
            )
            work[after:rank, start:] -= update
    out_ref[...] = work[:, rank:].T[:owned]


def finish(gram, owned_rows, total_rows):
    owned, rank = owned_rows.shape
    width = rank + -(-owned // LANES) * LANES
    block = pl.BlockSpec(memory_space=pltpu.VMEM)
    return pl.pallas_call(
        functools.partial(finish_kernel, total_rows),
        out_shape=jax.ShapeDtypeStruct((owned, rank), jnp.float32),
        in_specs=[block] * 2,
        out_specs=block,
        scratch_shapes=[pltpu.VMEM((rank, width), jnp.float32)],
        compiler_params=pltpu.CompilerParams(vmem_limit_bytes=VMEM_LIMIT),
    )(gram, owned_rows)


def solution(mesh):
    n_wide, n_narrow = mesh.shape["wide"], mesh.shape["narrow"]
    owned = COLS_DEV

    def body(tile_values, tile_row, tile_col, basis):
        total_rows = owned * n_wide
        partial = local_terms(tile_values, tile_row, tile_col, basis, total_rows)
        gram, owned_rows = sum_and_gather(partial, n_wide, n_narrow)
        return finish(gram, owned_rows, total_rows)

    in_specs = (
        P(("wide", "narrow"), None, None),
        P(("wide", "narrow")),
        P(("wide", "narrow")),
        P(("wide", "narrow"), None),
    )
    return jax.shard_map(body, mesh=mesh, in_specs=in_specs, out_specs=P("wide", None), check_vma=False)
```

time: 57.9 us -> 51.1 us (0.88)
  Pallas kernels: 53.1 us -> 46.3 us
    pallas_call x1, Pallas kernels: 38.2 us -> 32.6 us  [sum_and_gather(): pl.pallas_call(functools.partial(sum_gather_kernel, n_narrow, orders), ou...]
    pallas_call x1, Pallas kernels: 11.7 us -> 10 us  [finish(): pl.pallas_call(functools.partial(finish_kernel, total_rows), out_shape=ja...]
where the time goes in v2:
time: 51.1 us; the launch traced here: 50.9 us
  Pallas kernels  46.3 us (91%)
  local copies, waits for them, and re-layouts  4.57 us (9%)
    pallas_call x1, Pallas kernels, sum_and_gather(): pl.pallas_call(functools.partial(sum_gather_kernel, n_narrow, orders), ou...  32.6 us
    pallas_call x1, Pallas kernels, finish(): pl.pallas_call(functools.partial(finish_kernel, total_rows), out_shape=ja...  10 us
    unnamed x8, local copies, waits for them, and re-layouts  4.57 us
    pallas_call x1, Pallas kernels, local_terms(): pl.pallas_call(local_kernel, out_shape=jax.ShapeDtypeStruct((total_rows,...  3.7 us

profile of v2, /device:TPU:0, one launch (start us, length us, event | category | flops | bytes accessed | tf_op | source)
XLA Modules:
  0.0 50.9 jit_solution(16785564694164427308)
XLA Ops:
  0.0 0.0 copy-start
  0.0 2.0 %copy-done = bf16[7,512,512]{2,1,0:T(8,128)(2,1)S(1)} copy-done((bf16[7,512,512]{2,1,0:T(8,128)(2,1)S(1)}, bf16[7,512,512]{2,1,0:T(8,128)(2,1)}, u32[]{:S(2)}) %copy-start) | copy-done | bytes 3670040
  2.0 0.0 copy-start.1
  2.0 1.2 %copy-done.1 = f32[1024,256]{1,0:T(8,128)S(1)} copy-done((f32[1024,256]{1,0:T(8,128)S(1)}, f32[1024,256]{1,0:T(8,128)}, u32[]{:S(2)}) %copy-start.1) | copy-done | bytes 1048600
  3.3 0.0 copy-start.2
  3.3 0.7 %copy-done.2 = s32[7]{0:T(128)S(1)} copy-done((s32[7]{0:T(128)S(1)}, s32[7]{0:T(128)}, u32[]{:S(2)}) %copy-start.2) | copy-done | bytes 52
  3.9 0.0 copy-start.3
  3.9 0.7 %copy-done.3 = s32[7]{0:T(128)S(1)} copy-done((s32[7]{0:T(128)S(1)}, s32[7]{0:T(128)}, u32[]{:S(2)}) %copy-start.3) | copy-done | bytes 52
  4.6 3.7 %shard_map.46 = f32[1024,256]{1,0:T(8,128)S(1)} custom-call(s32[7]{0:T(128)S(1)} %copy-done.2, s32[7]{0:T(128)S(1)} %copy-done.3, bf16[7,512,512]{2,1,0:T(8,128)(2,1)S(1)} %copy-done, f32[1024,256]{1,0:T(8,128)S(1)} %copy-done.1), custom_call_target="tpu_custom_call" | custom-call | tf_op jit(solution)/shard_map/pallas_call | solution.py:46
  8.3 32.6 %shard_map.47 = (f32[256,256]{1,0:T(8,128)S(1)}, f32[64,256]{1,0:T(8,128)S(1)}) custom-call(f32[8,2,2,32,256]{4,3,2,1,0:T(8,128)S(1)} %bitcast.1), custom_call_target="tpu_custom_call" | custom-call | tf_op jit(solution)/shard_map/pallas_call | solution.py:236
  40.9 10.0 %shard_map.48 = f32[64,256]{1,0:T(8,128)} custom-call(f32[256,256]{1,0:T(8,128)S(1)} %get-tuple-element.7.gram_ref, f32[64,256]{1,0:T(8,128)S(1)} %get-tuple-element.8.owned_ref), custom_call_target="tpu_custom_call" | custom-call | tf_op jit(solution)/shard_map/pallas_call | solution.py:330
Async XLA Ops:
  0.0 2.0 %copy-start = (bf16[7,512,512]{2,1,0:T(8,128)(2,1)S(1)}, bf16[7,512,512]{2,1,0:T(8,128)(2,1)}, u32[]{:S(2)}) copy-start(bf16[7,512,512]{2,1,0:T(8,128)(2,1)} %tile_hbm.1) | copy-start | bytes 11010052
  2.0 1.2 %copy-start.1 = (f32[1024,256]{1,0:T(8,128)S(1)}, f32[1024,256]{1,0:T(8,128)}, u32[]{:S(2)}) copy-start(f32[1024,256]{1,0:T(8,128)} %basis_hbm.1) | copy-start | bytes 3145732
  3.3 0.7 %copy-start.2 = (s32[7]{0:T(128)S(1)}, s32[7]{0:T(128)}, u32[]{:S(2)}) copy-start(s32[7]{0:T(128)} %row_hbm.1) | copy-start | bytes 88
  3.9 0.7 %copy-start.3 = (s32[7]{0:T(128)S(1)}, s32[7]{0:T(128)}, u32[]{:S(2)}) copy-start(s32[7]{0:T(128)} %col_hbm.1) | copy-start | bytes 88

commit v3 on v2

--- a/solution.py
+++ b/solution.py
@@ -9,56 +9,11 @@
 
 MESH = pl.DeviceIdType.MESH
 HIGHEST = lax.Precision.HIGHEST
-VMEM_LIMIT = 48 * 1024 * 1024
+VMEM_LIMIT = 62 * 1024 * 1024
+FINISH_LIMIT = 62 * 1024 * 1024
+HALVES = 2
 COLS_DEV = 64
 LANES = 128
-
-
-def local_kernel(row_hbm, col_hbm, tile_hbm, basis_hbm, out_ref, row_ref, col_ref, tiles, basis, rounded, sem, tile_sem):
-    count, edge, _ = tiles.shape
-    small = [
-        pltpu.make_async_copy(row_hbm, row_ref, sem.at[0]),
-        pltpu.make_async_copy(col_hbm, col_ref, sem.at[1]),
-        pltpu.make_async_copy(basis_hbm, basis, sem.at[2]),
-    ]
-    large = [pltpu.make_async_copy(tile_hbm.at[t], tiles.at[t], tile_sem.at[t]) for t in range(count)]
-    for copy in small + large:
-        copy.start()
-    out_ref[...] = jnp.zeros_like(out_ref)
-    for copy in small:
-        copy.wait()
-    rounded[...] = basis[...].astype(jnp.bfloat16)
-    for t in range(count):
-        large[t].wait()
-        r = pl.multiple_of(row_ref[t] * edge, edge)
-        c = pl.multiple_of(col_ref[t] * edge, edge)
-        out_ref[pl.ds(c, edge), :] += lax.dot_general(
-            tiles[t],
-            rounded[pl.ds(r, edge), :],
-            (((0,), (0,)), ((), ())),
-            preferred_element_type=jnp.float32,
-        )
-
-
-def local_terms(tile_values, tile_row, tile_col, basis, total_rows):
-    count = tile_values.shape[0]
-    rows, rank = basis.shape
-    return pl.pallas_call(
-        local_kernel,
-        out_shape=jax.ShapeDtypeStruct((total_rows, rank), jnp.float32),
-        in_specs=[pl.BlockSpec(memory_space=pltpu.HBM)] * 4,
-        out_specs=pl.BlockSpec(memory_space=pltpu.VMEM),
-        scratch_shapes=[
-            pltpu.SMEM((count,), jnp.int32),
-            pltpu.SMEM((count,), jnp.int32),
-            pltpu.VMEM(tile_values.shape, jnp.bfloat16),
-            pltpu.VMEM((rows, rank), jnp.float32),
-            pltpu.VMEM((rows, rank), jnp.bfloat16),
-            pltpu.SemaphoreType.DMA((3,)),
-            pltpu.SemaphoreType.DMA((count,)),
-        ],
-        compiler_params=pltpu.CompilerParams(vmem_limit_bytes=VMEM_LIMIT),
-    )(tile_row, tile_col, tile_values, basis)
 
 
 def stream_orders(n_wide, n_narrow, chunk_rows):
@@ -89,12 +44,14 @@
     return place
 
 
-def sum_gather_kernel(n_narrow, orders, part_ref, gram_ref, owned_ref, recvs, accs, rows_all, gram_own, gram_in, sems):
+def sum_gather_kernel(n_narrow, orders, row_ref, col_ref, tile_hbm, basis_hbm, gram_ref, owned_ref, *scratch):
+    tiles, basis, rounded, part, recv0, recvs, accs, rows_all, gram_own, gram_in, sems = scratch
     w, n = lax.axis_index("wide"), lax.axis_index("narrow")
     me = w * n_narrow + n
     steps, streams = len(orders[0]), len(orders)
     rows, rank = rows_all.shape[2], rows_all.shape[3]
-    send_sem, recv_sem, gather_send, gather_recv, gram_send, gram_recv = sems
+    basis_sem, tile_sem, core_send, core_recv, send_sem, recv_sem, gather_send, gather_recv, gram_send, gram_recv = sems
+    count, edge, strip = tiles.shape[1:]
 
     def partner(group, delta):
         other, digit = me, (me // 2 ** group[0]) % 2 ** len(group)
@@ -111,11 +68,10 @@
             device, _ = partner(group, delta)
             pl.semaphore_signal(barrier, inc=1, device_id=device, device_id_type=MESH)
             met += 1
-    pl.semaphore_wait(barrier, met)
 
     def block_of(step, s, digit):
         if step == 0:
-            return part_ref.at[:, digit, :, pl.ds(s * rows, rows)]
+            return part.at[:, :, :, digit, :, pl.ds(s * rows, rows)]
         return accs[s][step - 1].at[:, digit]
 
     def start_sum(step, s):
@@ -124,7 +80,7 @@
             device, digit = partner(group, delta)
             copy = pltpu.make_async_remote_copy(
                 src_ref=block_of(step, s, digit),
-                dst_ref=recvs[s][step].at[delta - 1],
+                dst_ref=recvs[s][step - 1].at[delta - 1],
                 send_sem=send_sem.at[step, s, delta - 1],
                 recv_sem=recv_sem.at[step, s, delta - 1],
                 device_id=device,
@@ -155,40 +111,93 @@
             copies.append(copy)
         return copies
 
-    flying = [start_sum(0, s) for s in range(streams)]
-    for step in range(steps):
+    copies = [pltpu.make_async_copy(basis_hbm, basis, basis_sem.at[0])]
+    for h in range(HALVES):
+        for t in range(count):
+            source = tile_hbm.at[t, :, pl.ds(h * strip, strip)]
+            copies.append(pltpu.make_async_copy(source, tiles.at[h, t], tile_sem.at[h, t]))
+    for copy in copies:
+        copy.start()
+    copies[0].wait()
+    rounded[...] = basis[...].astype(jnp.bfloat16).reshape(rounded.shape)
+    core, other = (me // 2 ** orders[0][0][0]) % 2, partner(orders[0][0], 1)
+    core_copies = []
+    for h in range(HALVES):
+        for t in range(count):
+            copies[1 + h * count + t].wait()
+            product = lax.dot_general(
+                tiles[h, t], rounded[row_ref[t]], (((0,), (0,)), ((), ())), preferred_element_type=jnp.float32
+            ).reshape(part.shape[2:])
+            for c in range(part.shape[0]):
+                term = jnp.where(col_ref[t] == c, product, 0.0)
+                part[c, h] = term if t == 0 else part[c, h] + term
+        if h == 0:
+            pl.semaphore_wait(barrier, met)
+        for c in range(part.shape[0]):
+            copy = pltpu.make_async_remote_copy(
+                src_ref=part.at[c, h, :, other[1]],
+                dst_ref=recv0.at[c, h],
+                send_sem=core_send.at[c, h],
+                recv_sem=core_recv.at[c, h],
+                device_id=other[0],
+                device_id_type=MESH,
+            )
+            copy.start()
+            core_copies.append(copy)
+    for copy in core_copies:
+        copy.wait()
+    flying = []
+    for s in range(streams):
+        total = block_of(0, s, core)[...] + recv0[:, :, :, :, s * rows : (s + 1) * rows]
+        accs[s][0][...] = total.reshape(accs[s][0].shape)
+        flying.append(start_sum(1, s))
+
+    for step in range(1, steps):
         for s in range(streams):
             group = orders[s][step]
             digit = (me // 2 ** group[0]) % 2 ** len(group)
             total = block_of(step, s, digit)[...]
             for delta, copy in enumerate(flying[s]):
                 copy.wait()
-                total = total + recvs[s][step][delta]
+                total = total + recvs[s][step - 1][delta]
             if step < steps - 1:
                 accs[s][step][...] = total.reshape(accs[s][step].shape)
                 flying[s] = start_sum(step + 1, s)
             else:
                 rows_all[s, pl.ds(place_of(orders[s], me), 1)] = total.reshape((1, rows, rank))
                 flying[s] = start_gather(step, s)
-    for step in range(steps - 1, 0, -1):
+    for step in range(steps - 1, 1, -1):
         for s in range(streams):
             for copy in flying[s]:
                 copy.wait()
-            if step > 1:
-                flying[s] = start_gather(step - 1, s)
-
-    held = rows_all[...].reshape(-1, rank)
-    device, _ = partner(orders[0][0], 1)
-    copies = []
-    for i, at in enumerate(range(0, rank, LANES)):
-        place = (slice(at, at + LANES), slice(at, rank))
-        gram_own[place] = lax.dot_general(
+            flying[s] = start_gather(step - 1, s)
+
+    def gram_block(held, at):
+        return lax.dot_general(
             held[:, at : at + LANES],
             held[:, at:],
             (((0,), (0,)), ((), ())),
             precision=HIGHEST,
             preferred_element_type=jnp.float32,
         )
+
+    early = streams // 2
+    for s in range(early):
+        for copy in flying[s]:
+            copy.wait()
+    if early:
+        held = rows_all[:early].reshape(-1, rank)
+        for at in range(0, rank, LANES):
+            gram_own[at : at + LANES, at:] = gram_block(held, at)
+    for s in range(early, streams):
+        for copy in flying[s]:
+            copy.wait()
+    held = rows_all[early:].reshape(-1, rank)
+    device, _ = other
+    copies = []
+    for i, at in enumerate(range(0, rank, LANES)):
+        late = gram_block(held, at)
+        gram_own[at : at + LANES, at:] = gram_own[at : at + LANES, at:] + late if early else late
         copy = pltpu.make_async_remote_copy(
             src_ref=gram_own.at[pl.ds(at, LANES), pl.ds(at, rank - at)],
             dst_ref=gram_in.at[pl.ds(at, LANES), pl.ds(at, rank - at)],
@@ -199,10 +208,10 @@
         )
         copy.start()
         copies.append(copy)
-    for other in range(n_narrow):
+    for number in range(n_narrow):
         for s in range(streams):
-            at = (other * streams + s) * rows
-            owned_ref[at : at + rows, :] = rows_all[s, place_of(orders[s], w * n_narrow + other)]
+            at = (number * streams + s) * rows
+            owned_ref[at : at + rows, :] = rows_all[s, place_of(orders[s], w * n_narrow + number)]
     for at, copy in zip(range(0, rank, LANES), copies):
         copy.wait()
         place = (slice(at, at + LANES), slice(at, rank))
@@ -211,8 +220,10 @@
             gram_ref[at : at + LANES, :at] = jnp.zeros((LANES, at), jnp.float32)
 
 
-def sum_and_gather(partial, n_wide, n_narrow):
-    total_rows, rank = partial.shape
+def sum_and_gather(tile_values, tile_row, tile_col, basis, n_wide, n_narrow):
+    count, edge, _ = tile_values.shape
+    held_rows, rank = basis.shape
+    total_rows = COLS_DEV * n_wide
     devices = n_wide * n_narrow
     chunk = total_rows // devices
     orders = stream_orders(n_wide, n_narrow, chunk)
@@ -221,17 +232,20 @@
     recvs, accs = [], []
     for order in orders:
         recv, acc = [], []
-        for step in range(steps):
+        for step in range(1, steps):
             up, size, down = split_sizes(order, step)
             recv.append(pltpu.VMEM((size - 1, up, down, rows, rank), jnp.float32))
-            if step > 0:
-                acc.append(pltpu.VMEM((up, size, down, rows, rank), jnp.float32))
+            acc.append(pltpu.VMEM((up, size, down, rows, rank), jnp.float32))
         recvs.append(recv)
         accs.append(acc)
     up, size, down = split_sizes(orders[0], 0)
-    block = pl.BlockSpec(memory_space=pltpu.VMEM)
+    col_blocks = total_rows // edge
+    strip = edge // HALVES
+    up = up // (col_blocks * HALVES)
     most = max(2 ** len(group) for group in orders[0]) - 1
-    sems = [pltpu.SemaphoreType.DMA((steps, streams, most))] * 4 + [pltpu.SemaphoreType.DMA((rank // LANES,))] * 2
+    dma = pltpu.SemaphoreType.DMA
+    sems = [dma((1,)), dma((HALVES, count))] + [dma((col_blocks, HALVES))] * 2
+    sems += [dma((steps, streams, most))] * 4 + [dma((rank // LANES,))] * 2
     square = pltpu.VMEM((rank, rank), jnp.float32)
     return pl.pallas_call(
         functools.partial(sum_gather_kernel, n_narrow, orders),
@@ -239,9 +253,14 @@
             jax.ShapeDtypeStruct((rank, rank), jnp.float32),
             jax.ShapeDtypeStruct((chunk * n_narrow, rank), jnp.float32),
         ],
-        in_specs=[block],
-        out_specs=[block] * 2,
+        in_specs=[pl.BlockSpec(memory_space=pltpu.SMEM)] * 2 + [pl.BlockSpec(memory_space=pl.ANY)] * 2,
+        out_specs=[pl.BlockSpec(memory_space=pltpu.VMEM)] * 2,
         scratch_shapes=[
+            pltpu.VMEM((HALVES, count, edge, strip), jnp.bfloat16),
+            pltpu.VMEM((held_rows, rank), jnp.float32),
+            pltpu.VMEM((held_rows // edge, edge, rank), jnp.bfloat16),
+            pltpu.VMEM((col_blocks, HALVES, up, size, down, chunk, rank), jnp.float32),
+            pltpu.VMEM((col_blocks, HALVES, up, down, chunk, rank), jnp.float32),
             recvs,
             accs,
             pltpu.VMEM((streams, devices // 2, rows, rank), jnp.float32),
@@ -250,7 +269,7 @@
             sems,
         ],
         compiler_params=pltpu.CompilerParams(collective_id=0, has_side_effects=True, vmem_limit_bytes=VMEM_LIMIT),
-    )(partial.reshape(up, size, down, chunk, rank))
+    )(tile_row, tile_col, tile_values, basis)
 
 
 PANEL = 8
@@ -333,19 +352,16 @@
         in_specs=[block] * 2,
         out_specs=block,
         scratch_shapes=[pltpu.VMEM((rank, width), jnp.float32)],
-        compiler_params=pltpu.CompilerParams(vmem_limit_bytes=VMEM_LIMIT),
+        compiler_params=pltpu.CompilerParams(vmem_limit_bytes=FINISH_LIMIT),
     )(gram, owned_rows)
 
 
 def solution(mesh):
     n_wide, n_narrow = mesh.shape["wide"], mesh.shape["narrow"]
-    owned = COLS_DEV
 
     def body(tile_values, tile_row, tile_col, basis):
-        total_rows = owned * n_wide
-        partial = local_terms(tile_values, tile_row, tile_col, basis, total_rows)
-        gram, owned_rows = sum_and_gather(partial, n_wide, n_narrow)
-        return finish(gram, owned_rows, total_rows)
+        gram, owned_rows = sum_and_gather(tile_values, tile_row, tile_col, basis, n_wide, n_narrow)
+        return finish(gram, owned_rows, COLS_DEV * n_wide)
 
     in_specs = (
         P(("wide", "narrow"), None, None),

time: 51.1 us -> 48.7 us (0.953)
  local copies, waits for them, and re-layouts: 4.57 us -> 0 us
  Pallas kernels: 46.3 us -> 48.5 us
    pallas_call x1, Pallas kernels: 32.6 us -> 37.5 us  [sum_and_gather(): pl.pallas_call(functools.partial(sum_gather_kernel, n_narrow, orders), ou...]
    unnamed x8 -> x0, local copies, waits for them, and re-layouts: 4.57 us -> none
    pallas_call x1 -> x0, Pallas kernels: 3.7 us -> none  [local_terms(): pl.pallas_call(local_kernel, out_shape=jax.ShapeDtypeStruct((total_rows,...]
    pallas_call x1, Pallas kernels: 10 us -> 11 us  [finish(): pl.pallas_call(functools.partial(finish_kernel, total_rows), out_shape=ja...]
where the time goes in v3:
time: 48.7 us; the launch traced here: 48.5 us
  Pallas kernels  48.5 us (100%)
    pallas_call x1, Pallas kernels, sum_and_gather(): pl.pallas_call(functools.partial(sum_gather_kernel, n_narrow, orders), ou...  37.5 us
    pallas_call x1, Pallas kernels, finish(): pl.pallas_call(functools.partial(finish_kernel, total_rows), out_shape=ja...  11 us

profile of v3, /device:TPU:0, one launch (start us, length us, event | category | flops | bytes accessed | tf_op | source)
XLA Modules:
  0.0 48.5 jit_solution(12685970912104421211)
XLA Ops:
  0.0 37.5 %shard_map.46 = (f32[256,256]{1,0:T(8,128)}, f32[64,256]{1,0:T(8,128)}) custom-call(s32[7]{0:T(128)} %row_ref.1, s32[7]{0:T(128)} %col_ref.1, bf16[7,512,512]{2,1,0:T(8,128)(2,1)} %tile_hbm.1, f32[1024,256]{1,0:T(8,128)} %basis_hbm.1), custom_call_target="tpu_custom_call" | custom-call | tf_op jit(solution)/shard_map/pallas_call | solution.py:250
  37.5 11.0 %shard_map.47 = f32[64,256]{1,0:T(8,128)} custom-call(f32[256,256]{1,0:T(8,128)} %get-tuple-element.7.gram_ref, f32[64,256]{1,0:T(8,128)} %get-tuple-element.8.owned_ref), custom_call_target="tpu_custom_call" | custom-call | tf_op jit(solution)/shard_map/pallas_call | solution.py:349

commit v4 on v3

--- a/solution.py
+++ b/solution.py
@@ -273,7 +273,7 @@
 
 
 PANEL = 8
-OUTER = 32
+OUTER = 64
 
 
 def splat(value):
@@ -283,8 +283,15 @@
 def finish_kernel(total_rows, gram_ref, owned_ref, out_ref, work):
     owned, rank = owned_ref.shape
     width = work.shape[1]
-    work[:, :rank] = gram_ref[...] * (1.0 / total_rows)
-    filled = jnp.concatenate([owned_ref[...], jnp.zeros((width - rank - owned, rank), jnp.float32)], axis=0)
+    gram = gram_ref[...] * (1.0 / total_rows)
+    row = lax.broadcasted_iota(jnp.int32, gram.shape, 0)
+    diagonal = jnp.where(row == lax.broadcasted_iota(jnp.int32, gram.shape, 1), gram, 0.0)
+    across = lax.rsqrt(jnp.sum(diagonal, axis=0, keepdims=True))
+    down = lax.rsqrt(jnp.sum(diagonal, axis=1, keepdims=True))
+    work[:, :rank] = gram * across * down
+    filled = jnp.concatenate(
+        [owned_ref[...] * across, jnp.zeros((width - rank - owned, rank), jnp.float32)], axis=0
+    )
     work[:, rank:] = filled.T
 
     for outer in range(0, rank, OUTER):
@@ -299,13 +306,19 @@
             cols = [splat(head[:, k + j : k + j + 1]) for j in range(PANEL)]
             entry = [[splat(cols[j][i : i + 1, :]) for j in range(i + 1)] for i in range(PANEL)]
             scale = []
-            for j in range(PANEL):
-                scale.append(lax.rsqrt(entry[j][j]))
-                for i in range(j + 1, PANEL):
-                    entry[i][j] = entry[i][j] * scale[j]
-                for i in range(j + 1, PANEL):
-                    for m in range(j + 1, i + 1):
-                        entry[i][m] = entry[i][m] - entry[i][j] * entry[m][j]
+            for j in range(0, PANEL, 2):
+                a, b, c = entry[j][j], entry[j + 1][j], entry[j + 1][j + 1]
+                first = lax.rsqrt(a)
+                second = first * lax.rsqrt(a * c - b * b)
+                scale += [first, a * second]
+                for i in range(j + 2, PANEL):
+                    x, y = entry[i][j], entry[i][j + 1]
+                    entry[i][j], entry[i][j + 1] = x * first, (y * a - x * b) * second
+                entry[j + 1][j] = b * first
+                for i in range(j + 2, PANEL):
+                    for m in range(j + 2, i + 1):
+                        drop = entry[i][j] * entry[m][j] + entry[i][j + 1] * entry[m][j + 1]
+                        entry[i][m] = entry[i][m] - drop
             solved = [[splat(block[j : j + 1, :]) for block in groups[p]] for j in range(PANEL)]
             for j in range(PANEL):
                 solved[j] = [v * scale[j] for v in solved[j]]

time: 48.7 us -> 48.2 us (0.990)
  Pallas kernels: 48.5 us -> 48 us
where the time goes in v4:
time: 48.2 us; the launch traced here: 48 us
  Pallas kernels  48 us (100%)
    pallas_call x1, Pallas kernels, sum_and_gather(): pl.pallas_call(functools.partial(sum_gather_kernel, n_narrow, orders), ou...  37.5 us
    pallas_call x1, Pallas kernels, finish(): pl.pallas_call(functools.partial(finish_kernel, total_rows), out_shape=ja...  10.5 us

profile of v4, /device:TPU:0, one launch (start us, length us, event | category | flops | bytes accessed | tf_op | source)
XLA Modules:
  0.0 48.0 jit_solution(5509913997837224891)
XLA Ops:
  0.0 37.5 %shard_map.46 = (f32[256,256]{1,0:T(8,128)}, f32[64,256]{1,0:T(8,128)}) custom-call(s32[7]{0:T(128)} %row_ref.1, s32[7]{0:T(128)} %col_ref.1, bf16[7,512,512]{2,1,0:T(8,128)(2,1)} %tile_hbm.1, f32[1024,256]{1,0:T(8,128)} %basis_hbm.1), custom_call_target="tpu_custom_call" | custom-call | tf_op jit(solution)/shard_map/pallas_call | solution.py:250
  37.5 10.5 %shard_map.47 = f32[64,256]{1,0:T(8,128)} custom-call(f32[256,256]{1,0:T(8,128)} %get-tuple-element.7.gram_ref, f32[64,256]{1,0:T(8,128)} %get-tuple-element.8.owned_ref), custom_call_target="tpu_custom_call" | custom-call | tf_op jit(solution)/shard_map/pallas_call | solution.py:362

commit v5 on v4

--- a/solution.py
+++ b/solution.py
@@ -20,13 +20,15 @@
     nb = n_narrow.bit_length() - 1
     wb = n_wide.bit_length() - 1
     core = [(nb,)]
-    narrow = [(i,) for i in range(nb)]
-    second = [(nb + i,) for i in range(1, min(wb, 2))]
+    plane = [tuple(range(max(nb - 1, 0), nb)) + tuple(range(nb + 1, nb + min(wb, 2)))]
+    narrow = [(i,) for i in range(nb - 1)]
     rest = [tuple(range(nb + i, min(nb + i + 2, nb + wb))) for i in range(2, wb, 2)]
-    pair = [core + narrow + second + rest, core + second + narrow + rest]
-    if chunk_rows % 32 == 0:
-        return pair + pair
-    return pair if chunk_rows % 16 == 0 else pair[:1]
+    order = core + plane + narrow + rest
+    return [order] * (4 if chunk_rows % 32 == 0 else 2 if chunk_rows % 16 == 0 else 1)
+
+
+def digit_of(number, group):
+    return sum(((number // 2**b) % 2) * 2**i for i, b in enumerate(group))
 
 
 def split_sizes(order, step):
@@ -39,7 +41,7 @@
 def place_of(order, number):
     place, scale = 0, 1
     for group in reversed(order[1:]):
-        place = place + ((number // 2 ** group[0]) % 2 ** len(group)) * scale
+        place = place + digit_of(number, group) * scale
         scale = scale * 2 ** len(group)
     return place
 
@@ -54,7 +56,7 @@
     count, edge, strip = tiles.shape[1:]
 
     def partner(group, delta):
-        other, digit = me, (me // 2 ** group[0]) % 2 ** len(group)
+        other, digit = me, digit_of(me, group)
         for i, b in enumerate(group):
             if (delta >> i) & 1:
                 turn = 1 - 2 * ((me // 2**b) % 2)
@@ -120,7 +122,7 @@
         copy.start()
     copies[0].wait()
     rounded[...] = basis[...].astype(jnp.bfloat16).reshape(rounded.shape)
-    core, other = (me // 2 ** orders[0][0][0]) % 2, partner(orders[0][0], 1)
+    core, other = digit_of(me, orders[0][0]), partner(orders[0][0], 1)
     core_copies = []
     for h in range(HALVES):
         for t in range(count):
@@ -155,7 +157,7 @@
     for step in range(1, steps):
         for s in range(streams):
             group = orders[s][step]
-            digit = (me // 2 ** group[0]) % 2 ** len(group)
+            digit = digit_of(me, group)
             total = block_of(step, s, digit)[...]
             for delta, copy in enumerate(flying[s]):
                 copy.wait()

time: 48.2 us -> 45.4 us (0.942)
  Pallas kernels: 48 us -> 45.2 us
    pallas_call x1, Pallas kernels: 37.5 us -> 34.7 us  [sum_and_gather(): pl.pallas_call(functools.partial(sum_gather_kernel, n_narrow, orders), ou...]
where the time goes in v5:
time: 45.4 us; the launch traced here: 45.2 us
  Pallas kernels  45.2 us (100%)
    pallas_call x1, Pallas kernels, sum_and_gather(): pl.pallas_call(functools.partial(sum_gather_kernel, n_narrow, orders), ou...  34.7 us
    pallas_call x1, Pallas kernels, finish(): pl.pallas_call(functools.partial(finish_kernel, total_rows), out_shape=ja...  10.5 us

profile of v5, /device:TPU:0, one launch (start us, length us, event | category | flops | bytes accessed | tf_op | source)
XLA Modules:
  0.0 45.2 jit_solution(10545393024695325582)
XLA Ops:
  0.0 34.7 %shard_map.46 = (f32[256,256]{1,0:T(8,128)}, f32[64,256]{1,0:T(8,128)}) custom-call(s32[7]{0:T(128)} %row_ref.1, s32[7]{0:T(128)} %col_ref.1, bf16[7,512,512]{2,1,0:T(8,128)(2,1)} %tile_hbm.1, f32[1024,256]{1,0:T(8,128)} %basis_hbm.1), custom_call_target="tpu_custom_call" | custom-call | tf_op jit(solution)/shard_map/pallas_call | solution.py:252
  34.7 10.5 %shard_map.47 = f32[64,256]{1,0:T(8,128)} custom-call(f32[256,256]{1,0:T(8,128)} %get-tuple-element.7.gram_ref, f32[64,256]{1,0:T(8,128)} %get-tuple-element.8.owned_ref), custom_call_target="tpu_custom_call" | custom-call | tf_op jit(solution)/shard_map/pallas_call | solution.py:364

commit v6 on v5

--- a/solution.py
+++ b/solution.py
@@ -70,6 +70,8 @@
             device, _ = partner(group, delta)
             pl.semaphore_signal(barrier, inc=1, device_id=device, device_id_type=MESH)
             met += 1
+
+    sent = []
 
     def block_of(step, s, digit):
         if step == 0:
@@ -89,6 +91,7 @@
                 device_id_type=MESH,
             )
             copy.start()
+            sent.append(copy)
             copies.append(copy)
         return copies
 
@@ -110,6 +113,7 @@
                 device_id_type=MESH,
             )
             copy.start()
+            sent.append(copy)
             copies.append(copy)
         return copies
 
@@ -145,9 +149,10 @@
                 device_id_type=MESH,
             )
             copy.start()
+            sent.append(copy)
             core_copies.append(copy)
     for copy in core_copies:
-        copy.wait()
+        copy.wait_recv()
     flying = []
     for s in range(streams):
         total = block_of(0, s, core)[...] + recv0[:, :, :, :, s * rows : (s + 1) * rows]
@@ -160,7 +165,7 @@
             digit = digit_of(me, group)
             total = block_of(step, s, digit)[...]
             for delta, copy in enumerate(flying[s]):
-                copy.wait()
+                copy.wait_recv()
                 total = total + recvs[s][step - 1][delta]
             if step < steps - 1:
                 accs[s][step][...] = total.reshape(accs[s][step].shape)
@@ -171,7 +176,7 @@
     for step in range(steps - 1, 1, -1):
         for s in range(streams):
             for copy in flying[s]:
-                copy.wait()
+                copy.wait_recv()
             flying[s] = start_gather(step - 1, s)
 
     def gram_block(held, at):
@@ -186,14 +191,14 @@
     early = streams // 2
     for s in range(early):
         for copy in flying[s]:
-            copy.wait()
+            copy.wait_recv()
     if early:
         held = rows_all[:early].reshape(-1, rank)
         for at in range(0, rank, LANES):
             gram_own[at : at + LANES, at:] = gram_block(held, at)
     for s in range(early, streams):
         for copy in flying[s]:
-            copy.wait()
+            copy.wait_recv()
     held = rows_all[early:].reshape(-1, rank)
     device, _ = other
     copies = []
@@ -209,17 +214,20 @@
             device_id_type=MESH,
         )
         copy.start()
+        sent.append(copy)
         copies.append(copy)
     for number in range(n_narrow):
         for s in range(streams):
             at = (number * streams + s) * rows
             owned_ref[at : at + rows, :] = rows_all[s, place_of(orders[s], w * n_narrow + number)]
     for at, copy in zip(range(0, rank, LANES), copies):
-        copy.wait()
+        copy.wait_recv()
         place = (slice(at, at + LANES), slice(at, rank))
         gram_ref[place] = gram_own[place] + gram_in[place]
         if at > 0:
             gram_ref[at : at + LANES, :at] = jnp.zeros((LANES, at), jnp.float32)
+    for copy in sent:
+        copy.wait_send()
 
 
 def sum_and_gather(tile_values, tile_row, tile_col, basis, n_wide, n_narrow):

time: 45.4 us -> 45.7 us (level)
  no operation moved by 1% of the time
where the time goes in v6:
time: 45.7 us; the launch traced here: 45.6 us
  Pallas kernels  45.6 us (100%)
    pallas_call x1, Pallas kernels, sum_and_gather(): pl.pallas_call(functools.partial(sum_gather_kernel, n_narrow, orders), ou...  35.1 us
    pallas_call x1, Pallas kernels, finish(): pl.pallas_call(functools.partial(finish_kernel, total_rows), out_shape=ja...  10.5 us

profile of v6, /device:TPU:0, one launch (start us, length us, event | category | flops | bytes accessed | tf_op | source)
XLA Modules:
  0.0 45.6 jit_solution(16614219689167453565)
XLA Ops:
  0.0 35.1 %shard_map.46 = (f32[256,256]{1,0:T(8,128)}, f32[64,256]{1,0:T(8,128)}) custom-call(s32[7]{0:T(128)} %row_ref.1, s32[7]{0:T(128)} %col_ref.1, bf16[7,512,512]{2,1,0:T(8,128)(2,1)} %tile_hbm.1, f32[1024,256]{1,0:T(8,128)} %basis_hbm.1), custom_call_target="tpu_custom_call" | custom-call | tf_op jit(solution)/shard_map/pallas_call | solution.py:260
  35.1 10.5 %shard_map.47 = f32[64,256]{1,0:T(8,128)} custom-call(f32[256,256]{1,0:T(8,128)} %get-tuple-element.7.gram_ref, f32[64,256]{1,0:T(8,128)} %get-tuple-element.8.owned_ref), custom_call_target="tpu_custom_call" | custom-call | tf_op jit(solution)/shard_map/pallas_call | solution.py:372
